TPU v7x, 512 devices: a whole 4x4x16 slice. The times are simulated.
512 devices in a mesh: seq: 32 (over x, z_lo, core), head: 16 (over y, z_hi).
Axes of the slice: x: 4, y: 4, z: 16 (z_hi: 4, z_lo: 4; z = z_hi * 4 + z_lo), core: 2. Of those that a mesh axis runs over, the one named last changes fastest.
Arguments:
- queries: bfloat16 [65536, 4096], P('seq', 'head'), may hold values from -24 to 24
- key_value_rows: bfloat16 [65536, 2048], P('seq', 'head'), may hold values from -4 to 4
- upstream: bfloat16 [65536, 4096], P('seq', 'head'), may hold values from -6 to 6
- ancestors: int32 [512, 2], P(('seq', 'head')), may hold values from -1 to 510, as said below
- valid: int32 [512, 2], P(('seq', 'head')), may hold values from 0 to 1
- span_lo: int32 [65536], P(('seq', 'head')), may hold values from 0 to 7, as said below
- span_hi: int32 [65536], P(('seq', 'head')), may hold values from 1 to 7, as said below
Outputs:
- grad_queries: bfloat16 [65536, 4096], P('seq', 'head')
- key_value_gradient: bfloat16 [65536, 2048], P('seq', 'head')
Inputs may be any that keep to these rules, and one draw needn't show every extreme that they name: For block b and slot a with valid[b, a] = 1, b - 6 <= ancestors[b, a] <= b - 1, and the valid entries of one block are distinct; entries with valid 0 hold -1. `span_lo`: inside each block the tokens form 8 nodes, each a run of consecutive tokens numbered in depth-first order from 0, the first node at least two tokens long and the root of the block's tree. span_lo[t] <= span_hi[t]; tokens of one node share both numbers.
All inputs are finite; a program needn't handle non-finite values.
Results may differ from a plain program's by a relative error of at most 0.02.
Values may be sent and summed in bfloat16 or wider, within the bound.
A program may use at most 64 MiB of HBM per device.

v0:
```python
import jax
import jax.numpy as jnp
from jax import lax
from jax.sharding import PartitionSpec as P

QUERY_HEADS = 32
KEY_VALUE_HEADS = 8
HEAD_SIZE = 128
SPAN = 6
NANC = 2


def passed_along(block, axis, distance):
    devices = range(lax.axis_size(axis))
    route = [(i - distance, i) for i in devices if i - distance in devices]
    return lax.ppermute(block, axis, route)


def attend_group(queries, upstream, keys, values, mask):
    count, heads, width_total = queries.shape
    factor = width_total ** (-0.5)
    plain = jnp.einsum("qrd,kd->rqk", queries, keys, preferred_element_type=jnp.float32)
    scores = jnp.where(mask[None], plain * factor, -jnp.inf)
    top = jnp.max(scores, axis=2, keepdims=True)
    exps = jnp.exp(scores - top)
    probs = exps / jnp.sum(exps, axis=2, keepdims=True)
    weights = probs.astype(jnp.bfloat16)
    output = jnp.einsum("rqk,kd->qrd", weights, values, preferred_element_type=jnp.float32).astype(
        jnp.bfloat16
    )
    delta = jnp.sum(upstream.astype(jnp.float32) * output.astype(jnp.float32), axis=2).T[:, :, None]
    sens = jnp.einsum("qrd,kd->rqk", upstream, values, preferred_element_type=jnp.float32)
    slopes = (probs * (sens - delta)).astype(jnp.bfloat16)
    query_grad = (
        jnp.einsum("rqk,kd->qrd", slopes, keys, preferred_element_type=jnp.float32) * factor
    )
    key_grad = (
        jnp.einsum("rqk,qrd->kd", slopes, queries, preferred_element_type=jnp.float32) * factor
    )
    value_grad = jnp.einsum("rqk,qrd->kd", weights, upstream, preferred_element_type=jnp.float32)
    return (query_grad, key_grad, value_grad)


def attend_tiles(queries, upstream, tile_keys, tile_value_rows, masks):
    keys = jnp.concatenate(tile_keys, axis=0)
    values = jnp.concatenate(tile_value_rows, axis=0)
    mask = jnp.concatenate(masks, axis=1)
    query_grad, key_grad, value_grad = attend_group(queries, upstream, keys, values, mask)
    rows = tile_keys[0].shape[0]
    key_grads = [key_grad[place * rows : (place + 1) * rows] for place in range(len(tile_keys))]
    value_grads = [value_grad[place * rows : (place + 1) * rows] for place in range(len(tile_keys))]
    return (query_grad, key_grads, value_grads)


def sequence_layout(queries, key_value_rows, upstream, ancestors, valid, span_lo, span_hi):
    local_query, local_pairs, local_upstream = (
        lax.all_to_all(queries, "head", split_axis=0, concat_axis=1, tiled=True),
        lax.all_to_all(key_value_rows, "head", split_axis=0, concat_axis=1, tiled=True),
        lax.all_to_all(upstream, "head", split_axis=0, concat_axis=1, tiled=True),
    )
    block = lax.axis_index(("seq", "head"))
    count = local_query.shape[0]
    fetched = [passed_along(local_pairs, ("seq", "head"), step) for step in range(1, SPAN + 1)]
    stacked = jnp.stack(fetched)
    offsets = block - ancestors[0]
    usable = valid[0] > 0
    chosen = [
        lax.dynamic_index_in_dim(
            stacked, jnp.clip(offsets[slot] - 1, 0, SPAN - 1), 0, keepdims=False
        )
        for slot in range(NANC)
    ]
    tile_stack = [local_pairs] + chosen
    order = jnp.arange(count)
    visible = (
        (order[None, :] <= order[:, None])
        & (span_lo[None, :] <= span_lo[:, None])
        & (span_lo[:, None] <= span_hi[None, :])
    )
    masks = [visible] + [jnp.broadcast_to(usable[slot], (count, count)) for slot in range(NANC)]
    head_group = QUERY_HEADS // KEY_VALUE_HEADS
    query_parts = []
    key_column_slice = []
    value_column_slice = []
    for head_index in range(KEY_VALUE_HEADS):
        queries_here = local_query[
            :, head_index * head_group * HEAD_SIZE : (head_index + 1) * head_group * HEAD_SIZE
        ].reshape(count, head_group, HEAD_SIZE)
        upstream_here = local_upstream[
            :, head_index * head_group * HEAD_SIZE : (head_index + 1) * head_group * HEAD_SIZE
        ].reshape(count, head_group, HEAD_SIZE)
        tile_keys = [
            current_tile[:, head_index * HEAD_SIZE : (head_index + 1) * HEAD_SIZE]
            for current_tile in tile_stack
        ]
        tile_value_rows = [
            current_tile[
                :,
                (KEY_VALUE_HEADS + head_index)
                * HEAD_SIZE : (KEY_VALUE_HEADS + head_index + 1)
                * HEAD_SIZE,
            ]
            for current_tile in tile_stack
        ]
        query_grad, key_grads, value_grads = attend_tiles(
            queries_here, upstream_here, tile_keys, tile_value_rows, masks
        )
        query_parts.append(query_grad.reshape(count, head_group * HEAD_SIZE))
        key_column_slice.append(key_grads)
        value_column_slice.append(value_grads)
    grads = [
        jnp.concatenate(
            [key_column_slice[head_index][place_index] for head_index in range(KEY_VALUE_HEADS)]
            + [
                value_column_slice[head_index][place_index] for head_index in range(KEY_VALUE_HEADS)
            ],
            axis=1,
        )
        for place_index in range(1 + NANC)
    ]
    parts = [
        sum(
            (
                jnp.where(usable[slot] & (offsets[slot] == step), grads[1 + slot], 0.0)
                for slot in range(NANC)
            )
        )
        for step in range(1, SPAN + 1)
    ]
    summed_terms = grads[0]
    for step in range(1, SPAN + 1):
        summed_terms = summed_terms + passed_along(parts[step - 1], ("seq", "head"), -step)
    grad_query = jnp.concatenate(query_parts, axis=1).astype(jnp.bfloat16)
    grad_pairs = summed_terms.astype(jnp.bfloat16)
    return (
        lax.all_to_all(grad_query, "head", split_axis=1, concat_axis=0, tiled=True),
        lax.all_to_all(grad_pairs, "head", split_axis=1, concat_axis=0, tiled=True),
    )


def on_device(queries, key_value_rows, upstream, ancestors, valid, span_lo, span_hi):
    return sequence_layout(queries, key_value_rows, upstream, ancestors, valid, span_lo, span_hi)


def solution(mesh):
    placed = (
        P("seq", "head"),
        P("seq", "head"),
        P("seq", "head"),
        P(("seq", "head"), None),
        P(("seq", "head"), None),
        P(("seq", "head")),
        P(("seq", "head")),
    )
    return jax.shard_map(
        on_device,
        mesh=mesh,
        in_specs=placed,
        out_specs=(P("seq", "head"), P("seq", "head")),
        check_vma=False,
    )
```

profile of v0, /device:TPU:64, one launch (start us, length us, event | category | flops | bytes accessed | tf_op | source)
XLA Modules:
  0.0 873.4 jit_solution(2135783421466625167)
XLA Ops:
  0.7 50.3 %all_to_all.92 = bf16[16,128,128]{2,1,0:T(8,128)(2,1)S(1)} all-to-all(bf16[16,128,128]{2,1,0:T(8,128)(2,1)} %bitcast.675), channel_id=1, replica_groups=mesh['seq'=32,'head'=16] {'head'}, dimensions={0} | all-to-all | bytes 1048576 | tf_op jit(solution)/shard_map/all_to_all | solution.py:58
  50.9 3.7 all-to-all-start.1
  64.5 7.6 collective-permute-start
  81.8 0.8 add_add_fusion
  82.6 7.3 collective-permute-start.1
  89.9 51.9 %all-to-all-done.1 = bf16[16,128,256]{2,1,0:T(8,128)(2,1)S(1)} async-done(((bf16[16,128,256]{2,1,0:T(8,128)(2,1)}), bf16[16,128,256]{2,1,0:T(8,128)(2,1)S(1)}, u32[]{:S(2)}, u32[]{:S(2)}) %all-to-all-start.1) | async-done | bytes 1048608 | tf_op jit(solution)/shard_map/all_to_all | solution.py:57
  141.8 6.7 all-to-all-start.2
  148.5 0.8 fusion.212
  149.3 13.4 %collective-permute-start.5 = (bf16[128,2048]{1,0:T(8,128)(2,1)S(1)}, bf16[128,2048]{1,0:T(8,128)(2,1)S(1)}, u32[]{:S(2)}, u32[]{:S(2)}) collective-permute-start(bf16[128,2048]{1,0:T(8,128)(2,1)S(1)} %copy_bitcast_fusion), channel_id=1, source_target_pairs={{0,6},{1,7},{2,8},{3,9},{4,10},{5,11},{6,12},{7,13},{8,14},{9,15},... | collective-permute-start | bytes 1572872 | tf_op jit(solution)/shard_map/ppermute | solution.py:16
  162.8 3.4 collective-permute-start.4
  166.2 3.1 collective-permute-start.3
  169.3 7.3 collective-permute-start.2
  176.7 1.1 bitcast_dynamic-update-slice_fusion.4
  177.7 51.8 %collective-permute-done.2 = bf16[128,2048]{1,0:T(8,128)(2,1)S(1)} collective-permute-done((bf16[128,2048]{1,0:T(8,128)(2,1)S(1)}, bf16[128,2048]{1,0:T(8,128)(2,1)S(1)}, u32[]{:S(2)}, u32[]{:S(2)}) %collective-permute-start.2) | collective-permute-done | bytes 524320 | tf_op jit(solution)/shard_map/ppermute | solution.py:16
  229.6 72.1 %collective-permute-done.3 = bf16[128,2048]{1,0:T(8,128)(2,1)S(1)} collective-permute-done((bf16[128,2048]{1,0:T(8,128)(2,1)S(1)}, bf16[128,2048]{1,0:T(8,128)(2,1)S(1)}, u32[]{:S(2)}, u32[]{:S(2)}) %collective-permute-start.3) | collective-permute-done | bytes 524320 | tf_op jit(solution)/shard_map/ppermute | solution.py:16
  301.9 0.8 fusion.213
  302.8 0.8 fusion.214
  304.2 0.9 fusion.210
  305.2 0.8 copy.223
  306.0 0.8 fusion.211
  306.8 1.2 fusion.224
  308.0 1.3 convolution_bitcast_fusion.8
  310.0 1.4 fusion.63
  312.1 1.3 convolution_bitcast_fusion.9
  314.6 1.3 fusion.222
  315.9 1.3 convolution_bitcast_fusion.10
  317.8 1.4 fusion.61
  319.6 1.3 fusion.221
  320.8 1.3 convolution_bitcast_fusion.11
  322.8 1.4 fusion.60
  324.6 1.2 fusion.220
  325.9 1.3 convolution_bitcast_fusion.12
  327.8 1.4 fusion.59
  329.3 1.0 fusion.76
  330.2 1.2 fusion.219
  331.5 1.3 convolution_bitcast_fusion.13
  333.4 1.5 fusion.58
  335.0 1.0 fusion.77
  336.0 2.1 fusion.218
  338.1 2.1 convolution_bitcast_fusion.14
  340.3 1.5 fusion.105
  341.7 1.5 fusion.57
  343.3 1.0 fusion.78
  344.3 2.2 fusion.217
  346.5 2.3 convolution_bitcast_fusion.15
  348.8 1.7 fusion.104
  350.6 1.8 fusion.56
  354.5 1.9 collective-permute-start.6
  356.5 48.0 %collective-permute-start.11 = (f32[128,2048]{0,1:T(8,128)S(1)}, f32[128,2048]{0,1:T(8,128)S(1)}, u32[]{:S(2)}, u32[]{:S(2)}) collective-permute-start(f32[128,2048]{0,1:T(8,128)S(1)} %get-tuple-element.5), channel_id=1, source_target_pairs={{6,0},{7,1},{8,2},{9,3},{10,4},{11,5},{12,6},{13,7},{14,8},{15,9},... | collective-permute-start | bytes 3145736 | tf_op jit(solution)/shard_map/ppermute | solution.py:16
  404.5 3.1 collective-permute-start.10
  407.6 2.6 collective-permute-start.9
  410.2 5.8 collective-permute-start.8
  416.1 3.3 collective-permute-start.7
  420.9 135.1 %collective-permute-done.11 = f32[128,2048]{0,1:T(8,128)S(1)} collective-permute-done((f32[128,2048]{0,1:T(8,128)S(1)}, f32[128,2048]{0,1:T(8,128)S(1)}, u32[]{:S(2)}, u32[]{:S(2)}) %collective-permute-start.11) | collective-permute-done | bytes 1048608 | tf_op jit(solution)/shard_map/ppermute | solution.py:16
  556.0 167.2 %collective-permute-done.10 = f32[128,2048]{0,1:T(8,128)S(1)} collective-permute-done((f32[128,2048]{0,1:T(8,128)S(1)}, f32[128,2048]{0,1:T(8,128)S(1)}, u32[]{:S(2)}, u32[]{:S(2)}) %collective-permute-start.10) | collective-permute-done | bytes 1048608 | tf_op jit(solution)/shard_map/ppermute | solution.py:16
  723.2 1.1 add_convert_fusion
  724.4 84.1 %all-to-all-start.4 = ((bf16[128,16,128]{0,2,1:T(8,128)(2,1)}), bf16[128,16,128]{0,2,1:T(8,128)(2,1)S(1)}, u32[]{:S(2)}, u32[]{:S(2)}) async-start(bf16[128,16,128]{0,2,1:T(8,128)(2,1)} %bitcast.146), calls=%async_computation.4 | async-start | bytes 1048576 | tf_op jit(solution)/shard_map/all_to_all | solution.py:137
  808.5 0.7 constant_dynamic-update-slice_fusion.6
  812.0 0.7 constant_dynamic-update-slice_fusion.2
  814.5 24.2 %all-to-all-done.4 = bf16[128,16,128]{0,2,1:T(8,128)(2,1)S(1)} async-done(((bf16[128,16,128]{0,2,1:T(8,128)(2,1)}), bf16[128,16,128]{0,2,1:T(8,128)(2,1)S(1)}, u32[]{:S(2)}, u32[]{:S(2)}) %all-to-all-start.4) | async-done | bytes 524320 | tf_op jit(solution)/shard_map/all_to_all | solution.py:137
  838.7 5.6 all-to-all-start.3
  844.3 1.0 copy.288
  845.3 26.8 %all-to-all-done.3 = bf16[128,16,256]{0,2,1:T(8,128)(2,1)S(1)} async-done(((bf16[128,16,256]{0,2,1:T(8,128)(2,1)}), bf16[128,16,256]{0,2,1:T(8,128)(2,1)S(1)}, u32[]{:S(2)}, u32[]{:S(2)}) %all-to-all-start.3) | async-done | bytes 1048608 | tf_op jit(solution)/shard_map/all_to_all | solution.py:136
  872.1 1.3 copy.271
  (258 shorter events, 17.4 us)
Async XLA Ops:
  0.6 54.0 %copy-start.92 = (s32[1,2]{1,0:T(1,128)S(1)}, s32[1,2]{1,0:T(1,128)}, u32[]{:S(2)}) copy-start(s32[1,2]{1,0:T(1,128)} %param.10) | copy-start | bytes 28
  0.6 63.6 %copy-start.93 = (s32[1,2]{1,0:T(1,128)S(1)}, s32[1,2]{1,0:T(1,128)}, u32[]{:S(2)}) copy-start(s32[1,2]{1,0:T(1,128)} %param.11) | copy-start | bytes 28
  0.7 63.7 %copy-start.91 = (s32[128]{0:T(128)S(1)}, s32[128]{0:T(128)}, u32[]{:S(2)}) copy-start(s32[128]{0:T(128)} %param.13) | copy-start | bytes 1540
  0.7 63.7 %copy-start.90 = (s32[128]{0:T(128)S(1)}, s32[128]{0:T(128)}, u32[]{:S(2)}) copy-start(s32[128]{0:T(128)} %param.12) | copy-start | bytes 1540
  50.9 90.9 %all-to-all-start.1 = ((bf16[16,128,256]{2,1,0:T(8,128)(2,1)}), bf16[16,128,256]{2,1,0:T(8,128)(2,1)S(1)}, u32[]{:S(2)}, u32[]{:S(2)}) async-start(bf16[16,128,256]{2,1,0:T(8,128)(2,1)} %bitcast.664), calls=%async_computation.1 | async-start | bytes 2097152 | tf_op jit(solution)/shard_map/all_to_all | solution.py:57
  64.5 104.7 %collective-permute-start = (bf16[128,2048]{1,0:T(8,128)(2,1)S(1)}, bf16[128,2048]{1,0:T(8,128)(2,1)S(1)}, u32[]{:S(2)}, u32[]{:S(2)}) collective-permute-start(bf16[128,2048]{1,0:T(8,128)(2,1)S(1)} %copy_bitcast_fusion), channel_id=1, source_target_pairs={{0,1},{1,2},{2,3},{3,4},{4,5},{5,6},{6,7},{7,8},{8,9},{9,10},{10,1... | collective-permute-start | bytes 1572872 | tf_op jit(solution)/shard_map/ppermute | solution.py:16
  82.6 94.0 %collective-permute-start.1 = (bf16[128,2048]{1,0:T(8,128)(2,1)S(1)}, bf16[128,2048]{1,0:T(8,128)(2,1)}, u32[]{:S(2)}, u32[]{:S(2)}) collective-permute-start(bf16[128,2048]{1,0:T(8,128)(2,1)S(1)} %copy_bitcast_fusion), channel_id=1, source_target_pairs={{0,2},{1,3},{2,4},{3,5},{4,6},{5,7},{6,8},{7,9},{8,10},{9,11},{10,... | collective-permute-start | bytes 1572872 | tf_op jit(solution)/shard_map/ppermute | solution.py:16
  141.8 163.3 %all-to-all-start.2 = ((bf16[16,128,256]{2,1,0:T(8,128)(2,1)}), bf16[16,128,256]{2,1,0:T(8,128)(2,1)S(1)}, u32[]{:S(2)}, u32[]{:S(2)}) async-start(bf16[16,128,256]{2,1,0:T(8,128)(2,1)} %bitcast.665), calls=%async_computation.2 | async-start | bytes 2097152 | tf_op jit(solution)/shard_map/all_to_all | solution.py:59
  149.3 160.0 %copy-start.24 = (bf16[128,128]{1,0:T(8,128)(2,1)}, bf16[128,128]{1,0:T(8,128)(2,1)S(1)}, u32[]{:S(2)}) copy-start(bf16[128,128]{1,0:T(8,128)(2,1)S(1)} %get-tuple-element.26) | copy-start | bytes 98308
  149.3 164.1 %copy-start.26 = (bf16[128,128]{1,0:T(8,128)(2,1)}, bf16[128,128]{1,0:T(8,128)(2,1)S(1)}, u32[]{:S(2)}) copy-start(bf16[128,128]{1,0:T(8,128)(2,1)S(1)} %get-tuple-element.29) | copy-start | bytes 98308
  149.3 167.8 %copy-start.28 = (bf16[128,128]{1,0:T(8,128)(2,1)}, bf16[128,128]{1,0:T(8,128)(2,1)S(1)}, u32[]{:S(2)}) copy-start(bf16[128,128]{1,0:T(8,128)(2,1)S(1)} %get-tuple-element.31) | copy-start | bytes 98308
  149.3 172.8 %copy-start.30 = (bf16[128,128]{1,0:T(8,128)(2,1)}, bf16[128,128]{1,0:T(8,128)(2,1)S(1)}, u32[]{:S(2)}) copy-start(bf16[128,128]{1,0:T(8,128)(2,1)S(1)} %get-tuple-element.33) | copy-start | bytes 98308
  149.3 152.4 %collective-permute-start.5 = (bf16[128,2048]{1,0:T(8,128)(2,1)S(1)}, bf16[128,2048]{1,0:T(8,128)(2,1)S(1)}, u32[]{:S(2)}, u32[]{:S(2)}) collective-permute-start(bf16[128,2048]{1,0:T(8,128)(2,1)S(1)} %copy_bitcast_fusion), channel_id=1, source_target_pairs={{0,6},{1,7},{2,8},{3,9},{4,10},{5,11},{6,12},{7,13},{8,14},{9,15},... | collective-permute-start | bytes 1572872 | tf_op jit(solution)/shard_map/ppermute | solution.py:16
  162.8 138.9 %collective-permute-start.4 = (bf16[128,2048]{1,0:T(8,128)(2,1)S(1)}, bf16[128,2048]{1,0:T(8,128)(2,1)S(1)}, u32[]{:S(2)}, u32[]{:S(2)}) collective-permute-start(bf16[128,2048]{1,0:T(8,128)(2,1)S(1)} %copy_bitcast_fusion), channel_id=1, source_target_pairs={{0,5},{1,6},{2,7},{3,8},{4,9},{5,10},{6,11},{7,12},{8,13},{9,14},{... | collective-permute-start | bytes 1572872 | tf_op jit(solution)/shard_map/ppermute | solution.py:16
  166.2 135.5 %collective-permute-start.3 = (bf16[128,2048]{1,0:T(8,128)(2,1)S(1)}, bf16[128,2048]{1,0:T(8,128)(2,1)S(1)}, u32[]{:S(2)}, u32[]{:S(2)}) collective-permute-start(bf16[128,2048]{1,0:T(8,128)(2,1)S(1)} %copy_bitcast_fusion), channel_id=1, source_target_pairs={{0,4},{1,5},{2,6},{3,7},{4,8},{5,9},{6,10},{7,11},{8,12},{9,13},{1... | collective-permute-start | bytes 1572872 | tf_op jit(solution)/shard_map/ppermute | solution.py:16
  169.3 60.3 %collective-permute-start.2 = (bf16[128,2048]{1,0:T(8,128)(2,1)S(1)}, bf16[128,2048]{1,0:T(8,128)(2,1)S(1)}, u32[]{:S(2)}, u32[]{:S(2)}) collective-permute-start(bf16[128,2048]{1,0:T(8,128)(2,1)S(1)} %copy_bitcast_fusion), channel_id=1, source_target_pairs={{0,3},{1,4},{2,5},{3,6},{4,7},{5,8},{6,9},{7,10},{8,11},{9,12},{10... | collective-permute-start | bytes 1572872 | tf_op jit(solution)/shard_map/ppermute | solution.py:16
  305.1 12.0 %copy-start.10 = (bf16[128,512]{0,1:T(8,128)(2,1)}, bf16[128,512]{0,1:T(8,128)(2,1)S(1)}, u32[]{:S(2)}) copy-start(bf16[128,512]{0,1:T(8,128)(2,1)S(1)} %get-tuple-element.12) | copy-start | bytes 393220
  305.1 17.0 %copy-start.8 = (bf16[128,512]{0,1:T(8,128)(2,1)}, bf16[128,512]{0,1:T(8,128)(2,1)S(1)}, u32[]{:S(2)}) copy-start(bf16[128,512]{0,1:T(8,128)(2,1)S(1)} %get-tuple-element.13) | copy-start | bytes 393220
  306.8 26.0 %copy-start.23 = (bf16[128,512]{0,1:T(8,128)(2,1)}, bf16[128,512]{0,1:T(8,128)(2,1)S(1)}, u32[]{:S(2)}) copy-start(bf16[128,512]{0,1:T(8,128)(2,1)S(1)} %get-tuple-element.23) | copy-start | bytes 393220
  322.2 2.4 copy-start.7
  327.1 3.1 copy-start.6
  327.1 3.1 copy-start.38
  327.2 3.1 copy-start.61
  327.2 3.1 copy-start.66
  327.2 3.1 copy-start.70
  332.8 3.2 copy-start.4
  333.4 4.7 copy-start.22
  336.0 4.3 copy-start.34
  336.0 4.3 copy-start.59
  336.0 4.3 copy-start.64
  350.6 2.4 copy-start.21
  350.6 2.5 copy-start.20
  353.8 65.5 %copy-start.42 = (bf16[128,128]{1,0:T(8,128)(2,1)S(1)}, bf16[128,128]{1,0:T(8,128)(2,1)}, u32[]{:S(2)}) copy-start(bf16[128,128]{1,0:T(8,128)(2,1)} %get-tuple-element.41) | copy-start | bytes 98308
  353.8 65.5 %copy-start.63 = (bf16[128,128]{1,0:T(8,128)(2,1)S(1)}, bf16[128,128]{1,0:T(8,128)(2,1)}, u32[]{:S(2)}) copy-start(bf16[128,128]{1,0:T(8,128)(2,1)} %get-tuple-element.57) | copy-start | bytes 98308
  353.8 65.5 %copy-start.68 = (bf16[128,128]{1,0:T(8,128)(2,1)S(1)}, bf16[128,128]{1,0:T(8,128)(2,1)}, u32[]{:S(2)}) copy-start(bf16[128,128]{1,0:T(8,128)(2,1)} %get-tuple-element.73) | copy-start | bytes 98308
  353.9 66.5 %copy-start.39 = (bf16[128,128]{1,0:T(8,128)(2,1)S(1)}, bf16[128,128]{1,0:T(8,128)(2,1)}, u32[]{:S(2)}) copy-start(bf16[128,128]{1,0:T(8,128)(2,1)} %get-tuple-element.37) | copy-start | bytes 98308
  353.9 66.4 %copy-start.62 = (bf16[128,128]{1,0:T(8,128)(2,1)S(1)}, bf16[128,128]{1,0:T(8,128)(2,1)}, u32[]{:S(2)}) copy-start(bf16[128,128]{1,0:T(8,128)(2,1)} %get-tuple-element.53) | copy-start | bytes 98308
  353.9 66.4 %copy-start.67 = (bf16[128,128]{1,0:T(8,128)(2,1)S(1)}, bf16[128,128]{1,0:T(8,128)(2,1)}, u32[]{:S(2)}) copy-start(bf16[128,128]{1,0:T(8,128)(2,1)} %get-tuple-element.69) | copy-start | bytes 98308
  353.9 66.7 %copy-start.35 = (bf16[128,128]{1,0:T(8,128)(2,1)S(1)}, bf16[128,128]{1,0:T(8,128)(2,1)}, u32[]{:S(2)}) copy-start(bf16[128,128]{1,0:T(8,128)(2,1)} %get-tuple-element.39) | copy-start | bytes 98308
  353.9 66.7 %copy-start.60 = (bf16[128,128]{1,0:T(8,128)(2,1)S(1)}, bf16[128,128]{1,0:T(8,128)(2,1)}, u32[]{:S(2)}) copy-start(bf16[128,128]{1,0:T(8,128)(2,1)} %get-tuple-element.55) | copy-start | bytes 98308
  353.9 66.7 %copy-start.65 = (bf16[128,128]{1,0:T(8,128)(2,1)S(1)}, bf16[128,128]{1,0:T(8,128)(2,1)}, u32[]{:S(2)}) copy-start(bf16[128,128]{1,0:T(8,128)(2,1)} %get-tuple-element.71) | copy-start | bytes 98308
  354.5 61.5 %collective-permute-start.6 = (f32[128,2048]{0,1:T(8,128)S(1)}, f32[128,2048]{0,1:T(8,128)S(1)}, u32[]{:S(2)}, u32[]{:S(2)}) collective-permute-start(f32[128,2048]{0,1:T(8,128)S(1)} %get-tuple-element.4), channel_id=1, source_target_pairs={{1,0},{2,1},{3,2},{4,3},{5,4},{6,5},{7,6},{8,7},{9,8},{10,9},{11,1... | collective-permute-start | bytes 3145736 | tf_op jit(solution)/shard_map/ppermute | solution.py:16
  356.5 199.5 %collective-permute-start.11 = (f32[128,2048]{0,1:T(8,128)S(1)}, f32[128,2048]{0,1:T(8,128)S(1)}, u32[]{:S(2)}, u32[]{:S(2)}) collective-permute-start(f32[128,2048]{0,1:T(8,128)S(1)} %get-tuple-element.5), channel_id=1, source_target_pairs={{6,0},{7,1},{8,2},{9,3},{10,4},{11,5},{12,6},{13,7},{14,8},{15,9},... | collective-permute-start | bytes 3145736 | tf_op jit(solution)/shard_map/ppermute | solution.py:16
  404.5 318.7 %collective-permute-start.10 = (f32[128,2048]{0,1:T(8,128)S(1)}, f32[128,2048]{0,1:T(8,128)S(1)}, u32[]{:S(2)}, u32[]{:S(2)}) collective-permute-start(f32[128,2048]{0,1:T(8,128)S(1)} %get-tuple-element.6), channel_id=1, source_target_pairs={{5,0},{6,1},{7,2},{8,3},{9,4},{10,5},{11,6},{12,7},{13,8},{14,9},{... | collective-permute-start | bytes 3145736 | tf_op jit(solution)/shard_map/ppermute | solution.py:16
  407.6 315.6 %collective-permute-start.9 = (f32[128,2048]{0,1:T(8,128)S(1)}, f32[128,2048]{0,1:T(8,128)S(1)}, u32[]{:S(2)}, u32[]{:S(2)}) collective-permute-start(f32[128,2048]{0,1:T(8,128)S(1)} %get-tuple-element.7), channel_id=1, source_target_pairs={{4,0},{5,1},{6,2},{7,3},{8,4},{9,5},{10,6},{11,7},{12,8},{13,9},{1... | collective-permute-start | bytes 3145736 | tf_op jit(solution)/shard_map/ppermute | solution.py:16
  410.2 313.0 %collective-permute-start.8 = (f32[128,2048]{0,1:T(8,128)S(1)}, f32[128,2048]{0,1:T(8,128)S(1)}, u32[]{:S(2)}, u32[]{:S(2)}) collective-permute-start(f32[128,2048]{0,1:T(8,128)S(1)} %get-tuple-element.8), channel_id=1, source_target_pairs={{3,0},{4,1},{5,2},{6,3},{7,4},{8,5},{9,6},{10,7},{11,8},{12,9},{13... | collective-permute-start | bytes 3145736 | tf_op jit(solution)/shard_map/ppermute | solution.py:16
  416.1 307.1 %collective-permute-start.7 = (f32[128,2048]{0,1:T(8,128)S(1)}, f32[128,2048]{0,1:T(8,128)S(1)}, u32[]{:S(2)}, u32[]{:S(2)}) collective-permute-start(f32[128,2048]{0,1:T(8,128)S(1)} %get-tuple-element.9), channel_id=1, source_target_pairs={{2,0},{3,1},{4,2},{5,3},{6,4},{7,5},{8,6},{9,7},{10,8},{11,9},{12,... | collective-permute-start | bytes 3145736 | tf_op jit(solution)/shard_map/ppermute | solution.py:16
  723.2 86.7 %copy-start.33 = (bf16[128,128]{1,0:T(8,128)(2,1)S(1)}, bf16[128,128]{1,0:T(8,128)(2,1)}, u32[]{:S(2)}) copy-start(bf16[128,128]{1,0:T(8,128)(2,1)} %get-tuple-element.35) | copy-start | bytes 98308
  723.2 86.7 %copy-start.52 = (bf16[128,128]{1,0:T(8,128)(2,1)S(1)}, bf16[128,128]{1,0:T(8,128)(2,1)}, u32[]{:S(2)}) copy-start(bf16[128,128]{1,0:T(8,128)(2,1)} %get-tuple-element.51) | copy-start | bytes 98308
  723.2 86.7 %copy-start.58 = (bf16[128,128]{1,0:T(8,128)(2,1)S(1)}, bf16[128,128]{1,0:T(8,128)(2,1)}, u32[]{:S(2)}) copy-start(bf16[128,128]{1,0:T(8,128)(2,1)} %get-tuple-element.67) | copy-start | bytes 98308
  723.2 87.6 %copy-start.31 = (bf16[128,128]{1,0:T(8,128)(2,1)S(1)}, bf16[128,128]{1,0:T(8,128)(2,1)}, u32[]{:S(2)}) copy-start(bf16[128,128]{1,0:T(8,128)(2,1)} %copy-done.30) | copy-start | bytes 98308
  723.2 87.6 %copy-start.48 = (bf16[128,128]{1,0:T(8,128)(2,1)S(1)}, bf16[128,128]{1,0:T(8,128)(2,1)}, u32[]{:S(2)}) copy-start(bf16[128,128]{1,0:T(8,128)(2,1)} %get-tuple-element.49) | copy-start | bytes 98308
  723.2 87.6 %copy-start.56 = (bf16[128,128]{1,0:T(8,128)(2,1)S(1)}, bf16[128,128]{1,0:T(8,128)(2,1)}, u32[]{:S(2)}) copy-start(bf16[128,128]{1,0:T(8,128)(2,1)} %get-tuple-element.65) | copy-start | bytes 98308
  724.3 87.4 %copy-start.29 = (bf16[128,128]{1,0:T(8,128)(2,1)S(1)}, bf16[128,128]{1,0:T(8,128)(2,1)}, u32[]{:S(2)}) copy-start(bf16[128,128]{1,0:T(8,128)(2,1)} %copy-done.28) | copy-start | bytes 98308
  724.3 87.4 %copy-start.44 = (bf16[128,128]{1,0:T(8,128)(2,1)S(1)}, bf16[128,128]{1,0:T(8,128)(2,1)}, u32[]{:S(2)}) copy-start(bf16[128,128]{1,0:T(8,128)(2,1)} %get-tuple-element.47) | copy-start | bytes 98308
  724.3 87.4 %copy-start.54 = (bf16[128,128]{1,0:T(8,128)(2,1)S(1)}, bf16[128,128]{1,0:T(8,128)(2,1)}, u32[]{:S(2)}) copy-start(bf16[128,128]{1,0:T(8,128)(2,1)} %get-tuple-element.63) | copy-start | bytes 98308
  724.4 88.3 %copy-start.27 = (bf16[128,128]{1,0:T(8,128)(2,1)S(1)}, bf16[128,128]{1,0:T(8,128)(2,1)}, u32[]{:S(2)}) copy-start(bf16[128,128]{1,0:T(8,128)(2,1)} %copy-done.26) | copy-start | bytes 98308
  724.4 88.3 %copy-start.41 = (bf16[128,128]{1,0:T(8,128)(2,1)S(1)}, bf16[128,128]{1,0:T(8,128)(2,1)}, u32[]{:S(2)}) copy-start(bf16[128,128]{1,0:T(8,128)(2,1)} %get-tuple-element.45) | copy-start | bytes 98308
  724.4 88.3 %copy-start.50 = (bf16[128,128]{1,0:T(8,128)(2,1)S(1)}, bf16[128,128]{1,0:T(8,128)(2,1)}, u32[]{:S(2)}) copy-start(bf16[128,128]{1,0:T(8,128)(2,1)} %get-tuple-element.61) | copy-start | bytes 98308
  724.4 89.2 %copy-start.25 = (bf16[128,128]{1,0:T(8,128)(2,1)S(1)}, bf16[128,128]{1,0:T(8,128)(2,1)}, u32[]{:S(2)}) copy-start(bf16[128,128]{1,0:T(8,128)(2,1)} %copy-done.24) | copy-start | bytes 98308
  724.4 89.2 %copy-start.37 = (bf16[128,128]{1,0:T(8,128)(2,1)S(1)}, bf16[128,128]{1,0:T(8,128)(2,1)}, u32[]{:S(2)}) copy-start(bf16[128,128]{1,0:T(8,128)(2,1)} %get-tuple-element.42) | copy-start | bytes 98308
  724.4 89.2 %copy-start.46 = (bf16[128,128]{1,0:T(8,128)(2,1)S(1)}, bf16[128,128]{1,0:T(8,128)(2,1)}, u32[]{:S(2)}) copy-start(bf16[128,128]{1,0:T(8,128)(2,1)} %get-tuple-element.58) | copy-start | bytes 98308
  724.4 114.3 %all-to-all-start.4 = ((bf16[128,16,128]{0,2,1:T(8,128)(2,1)}), bf16[128,16,128]{0,2,1:T(8,128)(2,1)S(1)}, u32[]{:S(2)}, u32[]{:S(2)}) async-start(bf16[128,16,128]{0,2,1:T(8,128)(2,1)} %bitcast.146), calls=%async_computation.4 | async-start | bytes 1048576 | tf_op jit(solution)/shard_map/all_to_all | solution.py:137
  838.7 33.4 %all-to-all-start.3 = ((bf16[128,16,256]{0,2,1:T(8,128)(2,1)}), bf16[128,16,256]{0,2,1:T(8,128)(2,1)S(1)}, u32[]{:S(2)}, u32[]{:S(2)}) async-start(bf16[128,16,256]{0,2,1:T(8,128)(2,1)} %constant_dynamic-update-slice_fusion), calls=%async_computation.3 | async-start | bytes 2097152 | tf_op jit(solution)/shard_map/all_to_all | solution.py:136
  (46 other events, 73.1 us)
where the time goes:
time: 875 us; the launch traced here: 873 us
  waiting for transfers between devices  529 us (60%)
  starting transfers between devices  207 us (24%)
  blocking collectives  50.3 us (6%)
  matrix products  47.1 us (5%)
  between operations  18.9 us (2%)
  local copies, waits for them, and re-layouts  18.4 us (2%)
    ppermute x12, waiting for transfers between devices, passed_along(): return lax.ppermute(block, axis, route)  426 us
    ppermute x12, starting transfers between devices, passed_along(): return lax.ppermute(block, axis, route)  107 us
    all_to_all x1, starting transfers between devices, sequence_layout(): lax.all_to_all(grad_pairs, 'head', split_axis=1, concat_axis=0, tiled=True)  84.1 us
    all_to_all x1, waiting for transfers between devices, sequence_layout(): lax.all_to_all(queries, 'head', split_axis=0, concat_axis=1, tiled=True)  51.9 us
    all_to_all x1, blocking collectives, sequence_layout(): lax.all_to_all(key_value_rows, 'head', split_axis=0, concat_axis=1, tiled...  50.3 us
    all_to_all x1, waiting for transfers between devices, sequence_layout(): lax.all_to_all(grad_query, 'head', split_axis=1, concat_axis=0, tiled=True)  26.8 us
    all_to_all x1, waiting for transfers between devices, sequence_layout(): lax.all_to_all(grad_pairs, 'head', split_axis=1, concat_axis=0, tiled=True)  24.2 us
  transfers between devices with their start and end apart: 16, of which 7 were waited for; matrix products, arithmetic and copies ran while one was open for 2% of the time, Pallas kernels for 0%

commit v1 on v0

v1 whole, which is shorter than its diff:
```python
import functools
import math

import jax
import jax.numpy as jnp
from jax import lax
from jax.experimental import pallas as pl
from jax.experimental.pallas import tpu as pltpu
from jax.sharding import PartitionSpec as P

HEAD = 128
BLOCK = 128
SPAN = 6
MESH = pl.DeviceIdType.MESH
CHUNK = 256
VMEM_LIMIT = 48 * 1024 * 1024


def place():
    s, h = lax.axis_index("seq"), lax.axis_index("head")
    return s, h, h // 4, h % 4


def wait_for(ref, sem):
    pltpu.make_async_copy(ref, ref, sem).wait()


def gather_kernel(ns, nh, rows, kv_ref, lo_ref, hi_ref, anc_ref, val_ref, out_ref, meta_ref, buf,
                  load_sem, meta_send, meta_recv, right_send, left_send, chain_recv, y_send, kv_recv, halo_send,
                  halo_recv):
    s, h, y, zh = place()
    chunks = rows // CHUNK
    halo = SPAN * BLOCK
    first_halo = (rows - halo) // CHUNK
    halos = halo // CHUNK
    order = list(range(chunks))[::-1]
    after, before = (s + 1) % ns, (s + ns - 1) % ns

    mine = 2 * (((zh + 1) % 4) // 2) + zh // 3
    load = pltpu.make_async_copy(kv_ref, buf.at[mine], load_sem)
    load.start()

    barrier = pltpu.get_barrier_semaphore()
    for step in range(1, nh):
        pl.semaphore_signal(barrier, inc=1, device_id=(s, (h + step) % nh), device_id_type=MESH)
    pl.semaphore_signal(barrier, inc=1, device_id=(after, h), device_id_type=MESH)
    pl.semaphore_signal(barrier, inc=1, device_id=(before, h), device_id_type=MESH)

    lane = lax.broadcasted_iota(jnp.int32, (8, BLOCK), 1)
    row = lax.broadcasted_iota(jnp.int32, (8, BLOCK), 0)
    scalars = jnp.where(lane == 0, anc_ref[0, 0], 0) + jnp.where(lane == 1, anc_ref[0, 1], 0)
    scalars = scalars + jnp.where(lane == 2, val_ref[0, 0], 0) + jnp.where(lane == 3, val_ref[0, 1], 0)
    fields = jnp.where(row == 0, lo_ref[...], jnp.where(row == 1, hi_ref[...], scalars))
    meta_ref[h] = fields
    load.wait()
    pl.semaphore_wait(barrier, nh + 1)

    def part(c):
        return pl.ds(c * CHUNK, CHUNK)

    def right(c):
        return pltpu.make_async_remote_copy(
            src_ref=buf.at[2 * (zh % 2), part(c)], dst_ref=buf.at[0, part(c)],
            send_sem=right_send.at[c], recv_sem=chain_recv.at[0, c], device_id=(s, (h + 1) % nh), device_id_type=MESH)

    def left(c):
        return pltpu.make_async_remote_copy(
            src_ref=buf.at[2 - zh % 2, part(c)], dst_ref=buf.at[1, part(c)],
            send_sem=left_send.at[c], recv_sem=chain_recv.at[1, c], device_id=(s, (h + nh - 1) % nh),
            device_id_type=MESH)

    kind = y // 2

    def target(slot, c):
        return out_ref.at[kind, pl.ds(halo + c * CHUNK, CHUNK)]

    def along_y(slot, c):
        return pltpu.make_async_remote_copy(
            src_ref=buf.at[slot, part(c)], dst_ref=target(slot, c), send_sem=y_send.at[slot, c],
            recv_sem=kv_recv.at[kind, c], device_id=(s, (2 * (y % 2) + slot) * 4 + zh), device_id_type=MESH)

    def stay(slot, c):
        return pltpu.make_async_copy(buf.at[slot, part(c)], target(slot, c), kv_recv.at[kind, c])

    def to_next(which, c):
        return pltpu.make_async_remote_copy(
            src_ref=out_ref.at[which, pl.ds(halo + c * CHUNK, CHUNK)],
            dst_ref=out_ref.at[which, pl.ds((c - first_halo) * CHUNK, CHUNK)],
            send_sem=halo_send.at[which, c - first_halo], recv_sem=halo_recv.at[which, c - first_halo],
            device_id=(after, h), device_id_type=MESH)

    @pl.when(zh <= 1)
    def _():
        for c in order:
            right(c).start()

    @pl.when(zh >= 2)
    def _():
        for c in order:
            left(c).start()

    def meta_copy(step):
        return pltpu.make_async_remote_copy(
            src_ref=meta_ref.at[h], dst_ref=meta_ref.at[h], send_sem=meta_send.at[step - 1],
            recv_sem=meta_recv.at[step - 1], device_id=(s, (h + step) % nh), device_id_type=MESH)

    for step in range(1, nh):
        meta_copy(step).start()

    home = (0, 3)

    def finish(c):
        for which in range(2):
            wait_for(out_ref.at[which, pl.ds(halo + c * CHUNK, CHUNK)], kv_recv.at[which, c])
            if c >= first_halo:
                to_next(which, c).start()

    for place_in_order, c in enumerate(order):
        for slot in range(2):
            edge = 3 * slot
            relay = 2 - slot

            @pl.when(zh != edge)
            def _():
                wait_for(buf.at[slot, part(c)], chain_recv.at[slot, c])

            @pl.when(zh == relay)
            def _():
                (right if slot == 0 else left)(c).start()

            @pl.when(y == home[slot])
            def _():
                stay(slot, c).start()

            @pl.when(y != home[slot])
            def _():
                along_y(slot, c).start()

        if place_in_order >= 1:
            finish(order[place_in_order - 1])
    finish(order[-1])

    for which in range(2):
        for piece in range(halos):
            wait_for(out_ref.at[which, pl.ds(piece * CHUNK, CHUNK)], halo_recv.at[which, piece])
    for step in range(1, nh):
        source = (h + nh - step) % nh
        wait_for(meta_ref.at[source], meta_recv.at[step - 1])
    for step in range(1, nh):
        meta_copy(step).wait_send()
    for c in order:
        @pl.when(zh != 3)
        def _():
            right(c).wait_send()

        @pl.when(zh != 0)
        def _():
            left(c).wait_send()

        for slot in range(2):
            @pl.when(y != home[slot])
            def _():
                along_y(slot, c).wait_send()
    for which in range(2):
        for c in range(first_halo, chunks):
            to_next(which, c).wait_send()


def attend_kernel(count, meta_s, meta_v, q_ref, up_ref, kv_ref, dq_ref, dkv_ref, halo_ref, acc):
    s = lax.axis_index("seq")
    factor = HEAD ** -0.5
    scale = factor * math.log2(math.e)
    halo = SPAN * BLOCK
    acc[...] = jnp.zeros_like(acc)
    key_at = lax.broadcasted_iota(jnp.int32, (BLOCK, BLOCK), 0)
    query_at = lax.broadcasted_iota(jnp.int32, (BLOCK, BLOCK), 1)

    def visit(i, carry):
        rows = pl.ds(pl.multiple_of(i * BLOCK, BLOCK), BLOCK)
        tiles = [pl.ds(pl.multiple_of((i + SPAN) * BLOCK, BLOCK), BLOCK)]
        used = []
        for slot in range(2):
            ok = meta_s[i, 2, 2 + slot] > 0
            at = jnp.where(ok, meta_s[i, 2, slot] - s * count, i) + SPAN
            at = jnp.clip(at, 0, count + SPAN - 1)
            tiles.append(pl.ds(pl.multiple_of(at * BLOCK, BLOCK), BLOCK))
            used.append(ok)
        q = jnp.concatenate([q_ref[rows, :HEAD], q_ref[rows, HEAD:]], axis=0)
        up = jnp.concatenate([up_ref[rows, :HEAD], up_ref[rows, HEAD:]], axis=0)
        k = jnp.concatenate([kv_ref[0, t, :] for t in tiles], axis=0)
        v = jnp.concatenate([kv_ref[1, t, :] for t in tiles], axis=0)
        nt = (((1,), (1,)), ((), ()))
        tn = (((0,), (0,)), ((), ()))
        scores = lax.dot_general(k, q, nt, preferred_element_type=jnp.float32)
        sens = lax.dot_general(v, up, nt, preferred_element_type=jnp.float32)
        lo_row = meta_v[i, 0:1, :]
        hi_row = meta_v[i, 1:2, :].astype(jnp.float32)
        hi_col = jnp.broadcast_to(hi_row, (BLOCK, BLOCK)).T
        seen = (key_at <= query_at) & (lo_row.astype(jnp.float32) <= hi_col)
        seen = jnp.concatenate([seen, seen], axis=1)
        low = -jnp.inf
        scores = jnp.concatenate(
            [jnp.where(seen, scores[:BLOCK], low)]
            + [scores[BLOCK * (1 + n):BLOCK * (2 + n)] + jnp.where(used[n], 0.0, low) for n in range(2)], axis=0)
        top = jnp.max(scores, axis=0, keepdims=True)
        exps = jnp.exp2((scores - top) * scale)
        inverse = 1.0 / jnp.sum(exps, axis=0, keepdims=True)
        probs = exps * inverse
        delta = jnp.sum(probs * sens, axis=0, keepdims=True)
        weights = probs.astype(jnp.bfloat16)
        slopes = (probs * (sens - delta)).astype(jnp.bfloat16)
        dq = lax.dot_general(slopes, k, tn, preferred_element_type=jnp.float32) * factor
        dq_ref[rows, :HEAD] = dq[:BLOCK].astype(jnp.bfloat16)
        dq_ref[rows, HEAD:] = dq[BLOCK:].astype(jnp.bfloat16)
        dk = jnp.dot(slopes, q, preferred_element_type=jnp.float32)
        dv = jnp.dot(weights, up, preferred_element_type=jnp.float32)
        for n, t in enumerate(tiles):
            acc[0, t, :] += dk[n * BLOCK:(n + 1) * BLOCK]
            acc[1, t, :] += dv[n * BLOCK:(n + 1) * BLOCK]
        return carry

    lax.fori_loop(0, count, visit, 0)
    halo_ref[0] = (acc[0, :halo] * factor).astype(jnp.bfloat16)
    halo_ref[1] = acc[1, :halo].astype(jnp.bfloat16)
    dkv_ref[0] = (acc[0, halo:] * factor).astype(jnp.bfloat16)
    dkv_ref[1] = acc[1, halo:].astype(jnp.bfloat16)


def return_kernel(ns, nh, rows, dkv_ref, halo_ref, out_ref, part_buf, chain_buf, halo_in, halo_sum,
                  halo_send, halo_recv, y_send, y_recv, left_send, right_send, chain_recv):
    s, h, y, zh = place()
    chunks = rows // CHUNK
    halo = SPAN * BLOCK
    first_halo = (rows - halo) // CHUNK
    halos = halo // CHUNK
    after, before = (s + 1) % ns, (s + ns - 1) % ns

    barrier = pltpu.get_barrier_semaphore()
    for step in range(1, 4):
        pl.semaphore_signal(barrier, inc=1, device_id=(s, ((y + step) % 4) * 4 + zh), device_id_type=MESH)
    for step in (1, 3):
        pl.semaphore_signal(barrier, inc=1, device_id=(s, y * 4 + (zh + step) % 4), device_id_type=MESH)
    pl.semaphore_signal(barrier, inc=1, device_id=(after, h), device_id_type=MESH)
    pl.semaphore_signal(barrier, inc=1, device_id=(before, h), device_id_type=MESH)
    pl.semaphore_wait(barrier, 7)

    def part(c):
        return pl.ds(c * CHUNK, CHUNK)

    def to_before(which, piece):
        return pltpu.make_async_remote_copy(
            src_ref=halo_ref.at[which, part(piece)], dst_ref=halo_in.at[which, part(piece)],
            send_sem=halo_send.at[which, piece], recv_sem=halo_recv.at[which, piece],
            device_id=(before, h), device_id_type=MESH)

    for piece in range(halos):
        for which in range(2):
            to_before(which, piece).start()

    slot_of = y % 2

    def source(which, c):
        if c < first_halo:
            return dkv_ref.at[which, part(c)]
        return halo_sum.at[which, part(c - first_halo)]

    def along_y(which, c):
        return pltpu.make_async_remote_copy(
            src_ref=source(which, c), dst_ref=part_buf.at[slot_of, part(c)], send_sem=y_send.at[which, c],
            recv_sem=y_recv.at[slot_of, c], device_id=(s, (2 * which + y // 2) * 4 + zh), device_id_type=MESH)

    def stay(which, c):
        return pltpu.make_async_copy(source(which, c), part_buf.at[slot_of, part(c)], y_recv.at[slot_of, c])

    def left(c):
        return pltpu.make_async_remote_copy(
            src_ref=part_buf.at[0, part(c)], dst_ref=chain_buf.at[0, part(c)],
            send_sem=left_send.at[c], recv_sem=chain_recv.at[0, c], device_id=(s, (h + nh - 1) % nh),
            device_id_type=MESH)

    def right(c):
        return pltpu.make_async_remote_copy(
            src_ref=part_buf.at[1, part(c)], dst_ref=chain_buf.at[1, part(c)],
            send_sem=right_send.at[c], recv_sem=chain_recv.at[1, c], device_id=(s, (h + 1) % nh),
            device_id_type=MESH)

    home = (0, 3)

    def give(c):
        for which in range(2):
            if c >= first_halo:
                piece = c - first_halo
                wait_for(halo_in.at[which, part(piece)], halo_recv.at[which, piece])
                halo_sum[which, part(piece)] = (
                    dkv_ref[which, part(c)].astype(jnp.float32)
                    + halo_in[which, part(piece)].astype(jnp.float32)).astype(jnp.bfloat16)

            @pl.when(y == home[which])
            def _():
                stay(which, c).start()

            @pl.when(y != home[which])
            def _():
                along_y(which, c).start()

    def total(slot, c):
        return (part_buf[slot, part(c)].astype(jnp.float32)
                + chain_buf[slot, part(c)].astype(jnp.float32)).astype(jnp.bfloat16)

    for c in range(first_halo):
        give(c)

    def chain(c):
        for slot in range(2):
            wait_for(part_buf.at[slot, part(c)], y_recv.at[slot, c])

        @pl.when(zh % 2 == 1)
        def _():
            left(c).start()

        @pl.when(zh % 2 == 0)
        def _():
            right(c).start()

        @pl.when(zh == 2)
        def _():
            wait_for(chain_buf.at[0, part(c)], chain_recv.at[0, c])
            part_buf[0, part(c)] = total(0, c)
            left(c).start()

        @pl.when(zh == 1)
        def _():
            wait_for(chain_buf.at[1, part(c)], chain_recv.at[1, c])
            part_buf[1, part(c)] = total(1, c)
            right(c).start()

    def settle(c):
        @pl.when(zh <= 1)
        def _():
            wait_for(chain_buf.at[0, part(c)], chain_recv.at[0, c])

        @pl.when(zh >= 2)
        def _():
            wait_for(chain_buf.at[1, part(c)], chain_recv.at[1, c])

        @pl.when(zh == 0)
        def _():
            out_ref[part(c)] = total(0, c)

        @pl.when(zh == 1)
        def _():
            out_ref[part(c)] = chain_buf[0, part(c)]

        @pl.when(zh == 2)
        def _():
            out_ref[part(c)] = chain_buf[1, part(c)]

        @pl.when(zh == 3)
        def _():
            out_ref[part(c)] = total(1, c)

    for c in range(chunks):
        if c >= 1 and first_halo + c - 1 < chunks:
            give(first_halo + c - 1)
        chain(c)
    for c in range(chunks):
        settle(c)

    for piece in range(halos):
        for which in range(2):
            to_before(which, piece).wait_send()
    for c in range(chunks):
        for which in range(2):
            @pl.when(y != home[which])
            def _():
                along_y(which, c).wait_send()

        @pl.when(zh != 0)
        def _():
            left(c).wait_send()

        @pl.when(zh != 3)
        def _():
            right(c).wait_send()


def solution(mesh):
    ns, nh = mesh.shape["seq"], mesh.shape["head"]

    def on_device(queries, key_value_rows, upstream, ancestors, valid, span_lo, span_hi):
        rows = queries.shape[0]
        count = rows // BLOCK
        halo = SPAN * BLOCK
        chunks, halos = rows // CHUNK, halo // CHUNK
        vmem = pl.BlockSpec(memory_space=pltpu.VMEM)
        smem = pl.BlockSpec(memory_space=pltpu.SMEM)
        dma = pltpu.SemaphoreType.DMA
        kv, meta = pl.pallas_call(
            functools.partial(gather_kernel, ns, nh, rows),
            out_shape=(jax.ShapeDtypeStruct((2, halo + rows, HEAD), jnp.bfloat16),
                       jax.ShapeDtypeStruct((nh, 8, BLOCK), jnp.int32)),
            in_specs=[pl.BlockSpec(memory_space=pl.ANY), vmem, vmem, smem, smem],
            out_specs=(vmem, vmem),
            scratch_shapes=[
                pltpu.VMEM((3, rows, HEAD), jnp.bfloat16),
                dma, dma((nh - 1,)), dma((nh - 1,)), dma((chunks,)), dma((chunks,)), dma((2, chunks)),
                dma((2, chunks)), dma((2, chunks)), dma((2, halos)), dma((2, halos)),
            ],
            compiler_params=pltpu.CompilerParams(
                collective_id=0, has_side_effects=True, vmem_limit_bytes=VMEM_LIMIT),
            name="gather_units",
        )(key_value_rows, span_lo.reshape(1, BLOCK), span_hi.reshape(1, BLOCK), ancestors, valid)
        dq, dkv, dhalo = pl.pallas_call(
            functools.partial(attend_kernel, count),
            out_shape=(jax.ShapeDtypeStruct(queries.shape, jnp.bfloat16),
                       jax.ShapeDtypeStruct((2, rows, HEAD), jnp.bfloat16),
                       jax.ShapeDtypeStruct((2, halo, HEAD), jnp.bfloat16)),
            in_specs=[smem, vmem, vmem, vmem, vmem],
            out_specs=(vmem, vmem, vmem),
            scratch_shapes=[pltpu.VMEM((2, halo + rows, HEAD), jnp.float32)],
            compiler_params=pltpu.CompilerParams(vmem_limit_bytes=VMEM_LIMIT),
            name="attend",
        )(meta, meta, queries, upstream, kv)
        grad_pairs = pl.pallas_call(
            functools.partial(return_kernel, ns, nh, rows),
            out_shape=jax.ShapeDtypeStruct((rows, HEAD), jnp.bfloat16),
            in_specs=[vmem, vmem],
            out_specs=vmem,
            scratch_shapes=[
                pltpu.VMEM((2, rows, HEAD), jnp.bfloat16), pltpu.VMEM((2, rows, HEAD), jnp.bfloat16),
                pltpu.VMEM((2, halo, HEAD), jnp.bfloat16), pltpu.VMEM((2, halo, HEAD), jnp.bfloat16),
                dma((2, halos)), dma((2, halos)), dma((2, chunks)), dma((2, chunks)), dma((chunks,)),
                dma((chunks,)), dma((2, chunks)),
            ],
            compiler_params=pltpu.CompilerParams(
                collective_id=1, has_side_effects=True, vmem_limit_bytes=VMEM_LIMIT),
            name="return_units",
        )(dkv, dhalo)
        return dq, grad_pairs

    placed = (P("seq", "head"), P("seq", "head"), P("seq", "head"), P(("seq", "head"), None),
              P(("seq", "head"), None), P(("seq", "head")), P(("seq", "head")))
    return jax.shard_map(on_device, mesh=mesh, in_specs=placed, out_specs=(P("seq", "head"), P("seq", "head")),
                         check_vma=False)
```

time: 875 us -> 201 us (0.23)
  the two profiles are of different devices: /device:TPU:64 before, /device:TPU:112 now
where the time goes in v1:
time: 201 us; the launch traced here: 200 us
  Pallas kernels  193 us (96%)
  local copies, waits for them, and re-layouts  6.89 us (3%)
    pallas_call x1, Pallas kernels, on_device(): pl.pallas_call(functools.partial(gather_kernel, ns, nh, rows), out_shape=...  90.2 us
    pallas_call x1, Pallas kernels, on_device(): pl.pallas_call(functools.partial(return_kernel, ns, nh, rows), out_shape=...  86.7 us
    pallas_call x1, Pallas kernels, on_device(): pl.pallas_call(functools.partial(attend_kernel, count), out_shape=(jax.Sh...  15.9 us
    unnamed x15, local copies, waits for them, and re-layouts  6.89 us

profile of v1, /device:TPU:112, one launch (start us, length us, event | category | flops | bytes accessed | tf_op | source)
XLA Modules:
  0.0 200.3 jit_solution(4634333112574156806)
XLA Ops:
  0.6 0.0 copy-start.2
  0.6 1.0 copy-done.2
  1.7 0.0 copy-start.3
  1.7 0.7 copy-done.3
  2.3 0.0 copy-start.4
  2.3 0.7 copy-done.4
  3.0 0.0 copy-start.5
  3.0 0.7 copy-done.5
  3.6 0.0 copy-start.6
  3.6 0.7 copy-done.6
  4.3 90.2 %gather_units.1 = (bf16[2,2816,128]{2,1,0:T(8,128)(2,1)S(1)}, s32[16,8,128]{2,1,0:T(8,128)S(1)}) custom-call(bf16[2048,128]{1,0:T(8,128)(2,1)S(1)} %copy-done.2, s32[1,128]{1,0:T(1,128)S(1)} %bitcast.2, s32[1,128]{1,0:T(1,128)S(1)} %bitcast.3, s32[1,2]{1,0:T(1,128)S(1)} %copy-done.5, s32[1,2]{1,0:T(1,128)S(1)} %copy-done.6), custom_call_target="tpu_custom_call" | custom-call | tf_op jit(solution)/shard_map/gather_units/pallas_call | solution.py:398
  94.5 0.0 copy-start
  94.5 1.2 copy-done
  95.7 0.0 copy-start.1
  95.7 1.2 copy-done.1
  96.9 15.9 %attend.1 = (bf16[2048,256]{1,0:T(8,128)(2,1)}, bf16[2,2048,128]{2,1,0:T(8,128)(2,1)S(1)}, bf16[2,768,128]{2,1,0:T(8,128)(2,1)S(1)}) custom-call(s32[16,8,128]{2,1,0:T(8,128)S(1)} %get-tuple-element.7.meta_s.meta_v, s32[16,8,128]{2,1,0:T(8,128)S(1)} %get-tuple-element.7.meta_s.meta_v, bf16[2048,256]{1,0:T(8,128)(2,1)S(1)} %copy-done, ...), custom_call_target="tpu_custom_call" | custom-call | tf_op jit(solution)/shard_map/attend/pallas_call | solution.py:413
  112.8 86.7 %return_units.1 = bf16[2048,128]{1,0:T(8,128)(2,1)S(1)} custom-call(bf16[2,2048,128]{2,1,0:T(8,128)(2,1)S(1)} %get-tuple-element.10.dkv_ref, bf16[2,768,128]{2,1,0:T(8,128)(2,1)S(1)} %get-tuple-element.11.halo_ref), custom_call_target="tpu_custom_call" | custom-call | tf_op jit(solution)/shard_map/return_units/pallas_call | solution.py:424
  199.5 0.8 copy.10
Async XLA Ops:
  0.6 1.0 copy-start.2
  1.7 0.7 copy-start.3
  2.3 0.7 copy-start.4
  3.0 0.7 copy-start.5
  3.6 0.7 copy-start.6
  94.5 1.2 copy-start
  95.7 1.2 copy-start.1

commit v2 on v0

v2 whole, which is shorter than its diff:
```python
import functools
import math

import jax
import jax.numpy as jnp
from jax import lax
from jax.experimental import pallas as pl
from jax.experimental.pallas import tpu as pltpu
from jax.sharding import PartitionSpec as P

HEAD = 128
BLOCK = 128
SPAN = 6
MESH = pl.DeviceIdType.MESH
CHUNK = 128
WINDOW = 3
BACK_WINDOW = 3
ARRIVE, RELAYED, LANDED = 3, 5, 7
BACK_RELAY, BACK_END = 3, 5
VMEM_LIMIT = 60 * 1024 * 1024
HOME = (0, 3)


def wait_for(ref, sem):
    pltpu.make_async_copy(ref, ref, sem).wait()


def kernel(ns, nh, rows, kv_ref, q_hbm, up_hbm, lo_ref, hi_ref, anc_ref, val_ref, dq_ref, dkv_ref,
           unit, kv, meta, meta_s, q_ref, up_ref, acc, back, halo_out, halo_in, part_buf, chain_buf,
           load_sem, meta_z_send, meta_z_recv, meta_y_send, meta_y_recv,
           right_send, left_send, chain_recv, y_send, kv_recv, halo_send, halo_recv,
           hback_send, hback_recv, yb_send, yb_recv, bleft_send, bright_send, bchain_recv):
    s, h = lax.axis_index("seq"), lax.axis_index("head")
    y, zh = h // 4, h % 4
    n = rows // CHUNK
    halo = SPAN * BLOCK
    nhalo = halo // CHUNK
    after, before = (s + 1) % ns, (s + ns - 1) % ns
    factor = HEAD ** -0.5
    scale = factor * math.log2(math.e)

    def peer(py, pz):
        return (s, py * 4 + pz)

    def when(cond):
        return pl.when(cond)

    mine = 2 * (((zh + 1) % 4) // 2) + zh // 3
    load = pltpu.make_async_copy(kv_ref, unit.at[mine], load_sem.at[0])
    load.start()
    load_q = pltpu.make_async_copy(q_hbm, q_ref, load_sem.at[1])
    load_up = pltpu.make_async_copy(up_hbm, up_ref, load_sem.at[2])

    barrier = pltpu.get_barrier_semaphore()
    for step in range(1, 4):
        pl.semaphore_signal(barrier, inc=1, device_id=peer((y + step) % 4, zh), device_id_type=MESH)
        pl.semaphore_signal(barrier, inc=1, device_id=peer(y, (zh + step) % 4), device_id_type=MESH)
    pl.semaphore_signal(barrier, inc=1, device_id=(after, h), device_id_type=MESH)
    pl.semaphore_signal(barrier, inc=1, device_id=(before, h), device_id_type=MESH)

    block = s * nh + h
    lane = lax.broadcasted_iota(jnp.int32, (1, BLOCK), 1)
    away = [jnp.where(val_ref[0, a] > 0, block - anc_ref[0, a], 0) for a in range(2)]
    meta[h, :, 0:BLOCK] = lo_ref[...]
    meta[h, :, BLOCK:2 * BLOCK] = hi_ref[...]
    meta[h, :, 2 * BLOCK:] = jnp.where(lane == 0, away[0], 0) + jnp.where(lane == 1, away[1], 0)
    load.wait()
    pl.semaphore_wait(barrier, 8)

    def part(c):
        start = c * CHUNK
        return pl.ds(start if isinstance(start, int) else pl.multiple_of(start, CHUNK), CHUNK)

    def chunk_at(k):
        return n - 1 - k

    def back_at(g):
        return (2 * n - 1 - nhalo - g) % n

    def remote(src, dst, send, recv, to):
        return pltpu.make_async_remote_copy(
            src_ref=src, dst_ref=dst, send_sem=send, recv_sem=recv, device_id=to, device_id_type=MESH)

    def meta_z(step):
        return remote(meta.at[h], meta.at[h], meta_z_send.at[step - 1], meta_z_recv.at[step - 1],
                      peer(y, (zh + step) % 4))

    def meta_y(step):
        rows4 = pl.ds(4 * y, 4)
        return remote(meta.at[rows4], meta.at[rows4], meta_y_send.at[step - 1], meta_y_recv.at[step - 1],
                      peer((y + step) % 4, zh))

    def right(c):
        return remote(unit.at[2 * (zh % 2), part(c)], unit.at[0, part(c)], right_send.at[c], chain_recv.at[0, c],
                      (s, (h + 1) % nh))

    def left(c):
        return remote(unit.at[2 - zh % 2, part(c)], unit.at[1, part(c)], left_send.at[c], chain_recv.at[1, c],
                      (s, (h + nh - 1) % nh))

    kind = y // 2

    def landing(which, c):
        return kv.at[which, part(c + nhalo)]

    def along_y(slot, c):
        return remote(unit.at[slot, part(c)], landing(kind, c), y_send.at[slot, c], kv_recv.at[kind, c],
                      peer(2 * (y % 2) + slot, zh))

    def stay(slot, c):
        return pltpu.make_async_copy(unit.at[slot, part(c)], landing(kind, c), kv_recv.at[kind, c])

    def to_next(which, piece):
        return remote(landing(which, piece + n - nhalo), kv.at[which, part(piece)], halo_send.at[which, piece],
                      halo_recv.at[which, piece], (after, h))

    def to_before(which, piece):
        return remote(halo_out.at[which, part(piece)], halo_in.at[which, part(piece)], hback_send.at[which, piece],
                      hback_recv.at[which, piece], (before, h))

    bslot = y % 2

    def back_y(which, c):
        return remote(back.at[which, part(c)], part_buf.at[bslot, part(c)], yb_send.at[which, c],
                      yb_recv.at[bslot, c], peer(2 * which + y // 2, zh))

    def back_stay(which, c):
        return pltpu.make_async_copy(back.at[which, part(c)], part_buf.at[bslot, part(c)], yb_recv.at[bslot, c])

    def back_left(c):
        return remote(part_buf.at[0, part(c)], chain_buf.at[0, part(c)], bleft_send.at[c], bchain_recv.at[0, c],
                      (s, (h + nh - 1) % nh))

    def back_right(c):
        return remote(part_buf.at[1, part(c)], chain_buf.at[1, part(c)], bright_send.at[c], bchain_recv.at[1, c],
                      (s, (h + 1) % nh))

    def own_start(k):
        @when(zh <= 1)
        def _():
            right(chunk_at(k)).start()

        @when(zh >= 2)
        def _():
            left(chunk_at(k)).start()

    def own_sent(k):
        @when(zh <= 1)
        def _():
            right(chunk_at(k)).wait_send()

        @when(zh >= 2)
        def _():
            left(chunk_at(k)).wait_send()

    for step in range(1, 4):
        meta_z(step).start()
    load_q.start()
    load_up.start()
    acc[...] = jnp.zeros_like(acc)

    key_at = lax.broadcasted_iota(jnp.int32, (BLOCK, BLOCK), 0)
    query_at = lax.broadcasted_iota(jnp.int32, (BLOCK, BLOCK), 1)
    nt = (((1,), (1,)), ((), ()))
    tn = (((0,), (0,)), ((), ()))

    def visit(i):
        def tile(d):
            return pl.ds(pl.multiple_of((i + SPAN - d) * BLOCK, BLOCK), BLOCK)

        mine_rows = pl.ds(pl.multiple_of(i * BLOCK, BLOCK), BLOCK)
        off = [meta_s[i, 0, 2 * BLOCK + a] for a in range(2)]
        q = jnp.concatenate([q_ref[mine_rows, :HEAD], q_ref[mine_rows, HEAD:]], axis=0)
        up = jnp.concatenate([up_ref[mine_rows, :HEAD], up_ref[mine_rows, HEAD:]], axis=0)

        def listed(which):
            picked = [jnp.zeros((BLOCK, HEAD), jnp.bfloat16) for _ in range(2)]
            for d in range(1, SPAN + 1):
                here = kv[which, tile(d), :]
                picked = [jnp.where(off[a] == d, here, picked[a]) for a in range(2)]
            return jnp.concatenate([kv[which, tile(0), :]] + picked, axis=0)

        k, v = listed(0), listed(1)
        scores = lax.dot_general(k, q, nt, preferred_element_type=jnp.float32)
        sens = lax.dot_general(v, up, nt, preferred_element_type=jnp.float32)
        lo_row = meta[i, :, 0:BLOCK].astype(jnp.float32)
        hi_row = meta[i, :, BLOCK:2 * BLOCK].astype(jnp.float32)
        hi_col = jnp.broadcast_to(hi_row, (BLOCK, BLOCK)).T
        seen = (key_at <= query_at) & (lo_row <= hi_col)
        seen = jnp.concatenate([seen, seen], axis=1)
        low = -jnp.inf
        scores = jnp.concatenate(
            [jnp.where(seen, scores[:BLOCK], low)]
            + [scores[BLOCK * (1 + a):BLOCK * (2 + a)] + jnp.where(off[a] > 0, 0.0, low) for a in range(2)], axis=0)
        top = jnp.max(scores, axis=0, keepdims=True)
        exps = jnp.exp2((scores - top) * scale)
        inverse = 1.0 / jnp.sum(exps, axis=0, keepdims=True)
        probs = exps * inverse
        delta = jnp.sum(probs * sens, axis=0, keepdims=True)
        weights = probs.astype(jnp.bfloat16)
        slopes = (probs * (sens - delta)).astype(jnp.bfloat16)
        dq = lax.dot_general(slopes, k, tn, preferred_element_type=jnp.float32) * factor
        dq_ref[mine_rows, :HEAD] = dq[:BLOCK].astype(jnp.bfloat16)
        dq_ref[mine_rows, HEAD:] = dq[BLOCK:].astype(jnp.bfloat16)
        for which, (left_side, right_side) in enumerate(((slopes, q), (weights, up))):
            grad = jnp.dot(left_side, right_side, preferred_element_type=jnp.float32)
            acc[which, tile(0), :] += grad[:BLOCK]
            for d in range(1, SPAN + 1):
                term = jnp.where(off[1] == d, grad[2 * BLOCK:], 0.0)
                term = jnp.where(off[0] == d, grad[BLOCK:2 * BLOCK], term)
                acc[which, tile(d), :] += term

    def total(slot, c):
        return (part_buf[slot, part(c)].astype(jnp.float32)
                + chain_buf[slot, part(c)].astype(jnp.float32)).astype(jnp.bfloat16)

    def bown_start(g):
        j = back_at(g)

        @when(zh % 2 == 1)
        def _():
            back_left(j).start()

        @when(zh % 2 == 0)
        def _():
            back_right(j).start()

    def bown_sent(g):
        j = back_at(g)

        @when(zh % 2 == 1)
        def _():
            back_left(j).wait_send()

        @when(zh % 2 == 0)
        def _():
            back_right(j).wait_send()

    first_compute = nhalo + LANDED
    last_compute = first_compute + n - 1
    first_give = first_compute + nhalo
    first_back = first_give + 2
    backs = (last_compute - first_back) // 2 + 1
    steps = last_compute + 1 + n + BACK_END - backs

    def step(t, carry):
        @when((t >= WINDOW) & (t < n + WINDOW))
        def _():
            own_sent(t - WINDOW)

        @when(t < n)
        def _():
            own_start(t)

        for slot in range(2):
            k = t - jnp.where(zh == 3 - 3 * slot, RELAYED, ARRIVE)

            @when((k >= 0) & (k < n))
            def _():
                c = chunk_at(k)

                @when(zh != 3 * slot)
                def _():
                    wait_for(unit.at[slot, part(c)], chain_recv.at[slot, c])

                @when(zh == 2 - slot)
                def _():
                    (right if slot == 0 else left)(c).start()

                @when(y == HOME[slot])
                def _():
                    stay(slot, c).start()

                @when(y != HOME[slot])
                def _():
                    along_y(slot, c).start()

        u = jnp.where(t > last_compute, backs + t - last_compute - 1, (t - first_back) // 2)
        turn = (t > last_compute) | ((t >= first_back) & ((t - first_back) % 2 == 0))

        @when(t == 2)
        def _():
            for i in range(1, 4):
                wait_for(meta.at[y * 4 + (zh + 4 - i) % 4], meta_z_recv.at[i - 1])
            for i in range(1, 4):
                meta_y(i).start()

        @when(turn & (u >= BACK_WINDOW) & (u < n + BACK_WINDOW))
        def _():
            bown_sent(u - BACK_WINDOW)

        @when(turn & (u < n))
        def _():
            j = back_at(u)
            for slot in range(2):
                wait_for(part_buf.at[slot, part(j)], yb_recv.at[slot, j])
            bown_start(u)

        @when((t >= LANDED) & (t < n + LANDED))
        def _():
            k = t - LANDED
            c = chunk_at(k)
            for which in range(2):
                wait_for(landing(which, c), kv_recv.at[which, c])

            @when(k < nhalo)
            def _():
                for which in range(2):
                    to_next(which, nhalo - 1 - k).start()

        @when(t == first_compute)
        def _():
            for i in range(1, 4):
                wait_for(meta.at[pl.ds(4 * ((y + 4 - i) % 4), 4)], meta_y_recv.at[i - 1])
            copy = pltpu.make_async_copy(meta, meta_s, load_sem.at[3])
            copy.start()
            load_q.wait()
            load_up.wait()
            copy.wait()

        @when((t >= first_compute) & (t <= last_compute))
        def _():
            i = last_compute - t

            @when(i < nhalo)
            def _():
                for which in range(2):
                    wait_for(kv.at[which, part(i)], halo_recv.at[which, i])

            for b in range(CHUNK // BLOCK):
                visit(i * (CHUNK // BLOCK) + b)

        @when(t == last_compute)
        def _():
            for piece in range(nhalo)[::-1]:
                for which in range(2):
                    scaled = acc[which, part(piece)] * (factor if which == 0 else 1.0)
                    halo_out[which, part(piece)] = scaled.astype(jnp.bfloat16)
                    to_before(which, piece).start()

        @when(turn & (u >= BACK_RELAY) & (u < n + BACK_RELAY))
        def _():
            j = back_at(u - BACK_RELAY)

            @when(zh == 2)
            def _():
                wait_for(chain_buf.at[0, part(j)], bchain_recv.at[0, j])
                part_buf[0, part(j)] = total(0, j)
                back_left(j).start()

            @when(zh == 1)
            def _():
                wait_for(chain_buf.at[1, part(j)], bchain_recv.at[1, j])
                part_buf[1, part(j)] = total(1, j)
                back_right(j).start()

        gives_early = (t >= first_give) & (t < first_give + n - nhalo)
        gives_late = turn & (u + 2 >= n - nhalo) & (u + 2 < n)

        @when(gives_early | gives_late)
        def _():
            j = back_at(jnp.where(gives_late, u + 2, t - first_give))
            for which in range(2):
                scaled = acc[which, part(j + nhalo)] * (factor if which == 0 else 1.0)

                @when(j < n - nhalo)
                def _():
                    back[which, part(j)] = scaled.astype(jnp.bfloat16)

                @when(j >= n - nhalo)
                def _():
                    piece = j - (n - nhalo)
                    wait_for(halo_in.at[which, part(piece)], hback_recv.at[which, piece])
                    back[which, part(j)] = (
                        scaled + halo_in[which, part(piece)].astype(jnp.float32)).astype(jnp.bfloat16)

                @when(y == HOME[which])
                def _():
                    back_stay(which, j).start()

                @when(y != HOME[which])
                def _():
                    back_y(which, j).start()

        @when(turn & (u >= BACK_END))
        def _():
            j = back_at(u - BACK_END)

            @when(zh <= 1)
            def _():
                wait_for(chain_buf.at[0, part(j)], bchain_recv.at[0, j])

            @when(zh >= 2)
            def _():
                wait_for(chain_buf.at[1, part(j)], bchain_recv.at[1, j])

            @when(zh == 0)
            def _():
                dkv_ref[part(j)] = total(0, j)

            @when(zh == 1)
            def _():
                dkv_ref[part(j)] = chain_buf[0, part(j)]

            @when(zh == 2)
            def _():
                dkv_ref[part(j)] = chain_buf[1, part(j)]

            @when(zh == 3)
            def _():
                dkv_ref[part(j)] = total(1, j)

        return carry

    lax.fori_loop(0, steps, step, 0)

    for i in range(1, 4):
        meta_z(i).wait_send()
        meta_y(i).wait_send()

    def drain(k, carry):
        @when(zh == 2)
        def _():
            right(k).wait_send()
            back_left(k).wait_send()

        @when(zh == 1)
        def _():
            left(k).wait_send()
            back_right(k).wait_send()

        for slot in range(2):
            @when(y != HOME[slot])
            def _():
                along_y(slot, k).wait_send()
                back_y(slot, k).wait_send()

            @when(k < nhalo)
            def _():
                to_next(slot, k).wait_send()
                to_before(slot, k).wait_send()

        return carry

    lax.fori_loop(0, n, drain, 0)


def solution(mesh):
    ns, nh = mesh.shape["seq"], mesh.shape["head"]

    def on_device(queries, key_value_rows, upstream, ancestors, valid, span_lo, span_hi):
        rows = queries.shape[0]
        halo = SPAN * BLOCK
        n, nhalo = rows // CHUNK, halo // CHUNK
        hbm = pl.BlockSpec(memory_space=pl.ANY)
        vmem = pl.BlockSpec(memory_space=pltpu.VMEM)
        smem = pl.BlockSpec(memory_space=pltpu.SMEM)
        dma = pltpu.SemaphoreType.DMA
        bf16, f32 = jnp.bfloat16, jnp.float32
        return pl.pallas_call(
            functools.partial(kernel, ns, nh, rows),
            out_shape=(jax.ShapeDtypeStruct(queries.shape, bf16), jax.ShapeDtypeStruct((rows, HEAD), bf16)),
            in_specs=[hbm, hbm, hbm, vmem, vmem, smem, smem],
            out_specs=(vmem, vmem),
            scratch_shapes=[
                pltpu.VMEM((3, rows, HEAD), bf16), pltpu.VMEM((2, halo + rows, HEAD), bf16),
                pltpu.VMEM((nh, 1, 3 * BLOCK), jnp.int32), pltpu.SMEM((nh, 1, 3 * BLOCK), jnp.int32),
                pltpu.VMEM(queries.shape, bf16), pltpu.VMEM(queries.shape, bf16),
                pltpu.VMEM((2, halo + rows, HEAD), f32), pltpu.VMEM((2, rows, HEAD), bf16),
                pltpu.VMEM((2, halo, HEAD), bf16), pltpu.VMEM((2, halo, HEAD), bf16),
                pltpu.VMEM((2, rows, HEAD), bf16), pltpu.VMEM((2, rows, HEAD), bf16),
                dma((4,)), dma((3,)), dma((3,)), dma((3,)), dma((3,)),
                dma((n,)), dma((n,)), dma((2, n)), dma((2, n)), dma((2, n)), dma((2, nhalo)), dma((2, nhalo)),
                dma((2, nhalo)), dma((2, nhalo)), dma((2, n)), dma((2, n)), dma((n,)), dma((n,)), dma((2, n)),
            ],
            compiler_params=pltpu.CompilerParams(
                collective_id=0, has_side_effects=True, vmem_limit_bytes=VMEM_LIMIT),
            name="tree_attention",
        )(key_value_rows, queries, upstream, span_lo.reshape(1, BLOCK), span_hi.reshape(1, BLOCK), ancestors, valid)

    placed = (P("seq", "head"), P("seq", "head"), P("seq", "head"), P(("seq", "head"), None),
              P(("seq", "head"), None), P(("seq", "head")), P(("seq", "head")))
    return jax.shard_map(on_device, mesh=mesh, in_specs=placed, out_specs=(P("seq", "head"), P("seq", "head")),
                         check_vma=False)
```

time: 875 us -> 154 us (0.18)
  the two profiles are of different devices: /device:TPU:64 before, /device:TPU:198 now
where the time goes in v2:
time: 154 us; the launch traced here: 153 us
  Pallas kernels  150 us (97%)
  local copies, waits for them, and re-layouts  3.12 us (2%)
    pallas_call x1, Pallas kernels, on_device(): pl.pallas_call(functools.partial(kernel, ns, nh, rows), out_shape=(jax.Sh...  150 us
    unnamed x4, local copies, waits for them, and re-layouts  3.12 us

profile of v2, /device:TPU:198, one launch (start us, length us, event | category | flops | bytes accessed | tf_op | source)
XLA Modules:
  0.0 153.3 jit_solution(7336593343817916354)
XLA Ops:
  0.6 149.6 %tree_attention.1 = (bf16[2048,256]{1,0:T(8,128)(2,1)}, bf16[2048,128]{1,0:T(8,128)(2,1)}) custom-call(bf16[2048,128]{1,0:T(8,128)(2,1)} %kv_ref.1, bf16[2048,256]{1,0:T(8,128)(2,1)} %q_hbm.1, bf16[2048,256]{1,0:T(8,128)(2,1)} %up_hbm.1, s32[1,128]{1,0:T(1,128)} %bitcast.2, s32[1,128]{1,0:T(1,128)} %bitcast.3, s32[1,2]{1,0:T(1,128)} %anc_ref.1, s32[1,2]{1,0:T(1,128)} %val_ref.1), custom_call_target="tpu_custom_call" | custom-call | tf_op jit(solution)/shard_map/tree_attention/pallas_call | solution.py:460
  150.2 0.0 copy-start
  150.2 2.3 %copy.11 = bf16[2048,256]{1,0:T(8,128)(2,1)} copy(bf16[2048,256]{1,0:T(8,128)(2,1)} %get-tuple-element.4) | data formatting | bytes 2097152
  152.5 0.0 copy-done
  152.5 0.8 copy.12
Async XLA Ops:
  150.2 2.3 %copy-start = (bf16[2048,128]{1,0:T(8,128)(2,1)S(1)}, bf16[2048,128]{1,0:T(8,128)(2,1)}, u32[]{:S(2)}) copy-start(bf16[2048,128]{1,0:T(8,128)(2,1)} %get-tuple-element.5) | copy-start | bytes 1572868

commit v3 on v2

--- a/solution.py
+++ b/solution.py
@@ -12,11 +12,11 @@
 BLOCK = 128
 SPAN = 6
 MESH = pl.DeviceIdType.MESH
-CHUNK = 128
-WINDOW = 3
+CHUNK = 256
+WINDOW = 2
 BACK_WINDOW = 3
-ARRIVE, RELAYED, LANDED = 3, 5, 7
-BACK_RELAY, BACK_END = 3, 5
+ARRIVE, RELAYED, LANDED = 2, 3, 4
+BACK_RELAY, BACK_END = 2, 4
 VMEM_LIMIT = 60 * 1024 * 1024
 HOME = (0, 3)
 
@@ -110,13 +110,13 @@
     def stay(slot, c):
         return pltpu.make_async_copy(unit.at[slot, part(c)], landing(kind, c), kv_recv.at[kind, c])
 
-    def to_next(which, piece):
-        return remote(landing(which, piece + n - nhalo), kv.at[which, part(piece)], halo_send.at[which, piece],
-                      halo_recv.at[which, piece], (after, h))
-
-    def to_before(which, piece):
-        return remote(halo_out.at[which, part(piece)], halo_in.at[which, part(piece)], hback_send.at[which, piece],
-                      hback_recv.at[which, piece], (before, h))
+    def to_next(piece):
+        return remote(kv.at[:, part(piece + n)], kv.at[:, part(piece)], halo_send.at[piece], halo_recv.at[piece],
+                      (after, h))
+
+    def to_before(piece):
+        return remote(halo_out.at[:, part(piece)], halo_in.at[:, part(piece)], hback_send.at[piece],
+                      hback_recv.at[piece], (before, h))
 
     bslot = y % 2
 
@@ -305,8 +305,7 @@
 
             @when(k < nhalo)
             def _():
-                for which in range(2):
-                    to_next(which, nhalo - 1 - k).start()
+                to_next(nhalo - 1 - k).start()
 
         @when(t == first_compute)
         def _():
@@ -324,8 +323,7 @@
 
             @when(i < nhalo)
             def _():
-                for which in range(2):
-                    wait_for(kv.at[which, part(i)], halo_recv.at[which, i])
+                wait_for(kv.at[:, part(i)], halo_recv.at[i])
 
             for b in range(CHUNK // BLOCK):
                 visit(i * (CHUNK // BLOCK) + b)
@@ -336,7 +334,7 @@
                 for which in range(2):
                     scaled = acc[which, part(piece)] * (factor if which == 0 else 1.0)
                     halo_out[which, part(piece)] = scaled.astype(jnp.bfloat16)
-                    to_before(which, piece).start()
+                to_before(piece).start()
 
         @when(turn & (u >= BACK_RELAY) & (u < n + BACK_RELAY))
         def _():
@@ -360,6 +358,12 @@
         @when(gives_early | gives_late)
         def _():
             j = back_at(jnp.where(gives_late, u + 2, t - first_give))
+
+            @when(j >= n - nhalo)
+            def _():
+                piece = j - (n - nhalo)
+                wait_for(halo_in.at[:, part(piece)], hback_recv.at[piece])
+
             for which in range(2):
                 scaled = acc[which, part(j + nhalo)] * (factor if which == 0 else 1.0)
 
@@ -370,7 +374,6 @@
                 @when(j >= n - nhalo)
                 def _():
                     piece = j - (n - nhalo)
-                    wait_for(halo_in.at[which, part(piece)], hback_recv.at[which, piece])
                     back[which, part(j)] = (
                         scaled + halo_in[which, part(piece)].astype(jnp.float32)).astype(jnp.bfloat16)
 
@@ -435,10 +438,10 @@
                 along_y(slot, k).wait_send()
                 back_y(slot, k).wait_send()
 
-            @when(k < nhalo)
-            def _():
-                to_next(slot, k).wait_send()
-                to_before(slot, k).wait_send()
+        @when(k < nhalo)
+        def _():
+            to_next(k).wait_send()
+            to_before(k).wait_send()
 
         return carry
 
@@ -470,8 +473,8 @@
                 pltpu.VMEM((2, halo, HEAD), bf16), pltpu.VMEM((2, halo, HEAD), bf16),
                 pltpu.VMEM((2, rows, HEAD), bf16), pltpu.VMEM((2, rows, HEAD), bf16),
                 dma((4,)), dma((3,)), dma((3,)), dma((3,)), dma((3,)),
-                dma((n,)), dma((n,)), dma((2, n)), dma((2, n)), dma((2, n)), dma((2, nhalo)), dma((2, nhalo)),
-                dma((2, nhalo)), dma((2, nhalo)), dma((2, n)), dma((2, n)), dma((n,)), dma((n,)), dma((2, n)),
+                dma((n,)), dma((n,)), dma((2, n)), dma((2, n)), dma((2, n)), dma((nhalo,)), dma((nhalo,)),
+                dma((nhalo,)), dma((nhalo,)), dma((2, n)), dma((2, n)), dma((n,)), dma((n,)), dma((2, n)),
             ],
             compiler_params=pltpu.CompilerParams(
                 collective_id=0, has_side_effects=True, vmem_limit_bytes=VMEM_LIMIT),

time: 154 us -> 149 us (0.968)
  the two profiles are of different devices: /device:TPU:198 before, /device:TPU:129 now
where the time goes in v3:
time: 149 us
  Pallas kernels  145 us (97%)
  local copies, waits for them, and re-layouts  3.12 us (2%)
    pallas_call x1, Pallas kernels, on_device(): pl.pallas_call(functools.partial(kernel, ns, nh, rows), out_shape=(jax.Sh...  145 us
    unnamed x4, local copies, waits for them, and re-layouts  3.12 us

profile of v3, /device:TPU:129, one launch (start us, length us, event | category | flops | bytes accessed | tf_op | source)
XLA Modules:
  0.0 149.0 jit_solution(6364311908077836008)
XLA Ops:
  0.6 145.2 %tree_attention.1 = (bf16[2048,256]{1,0:T(8,128)(2,1)}, bf16[2048,128]{1,0:T(8,128)(2,1)}) custom-call(bf16[2048,128]{1,0:T(8,128)(2,1)} %kv_ref.1, bf16[2048,256]{1,0:T(8,128)(2,1)} %q_hbm.1, bf16[2048,256]{1,0:T(8,128)(2,1)} %up_hbm.1, s32[1,128]{1,0:T(1,128)} %bitcast.2, s32[1,128]{1,0:T(1,128)} %bitcast.3, s32[1,2]{1,0:T(1,128)} %anc_ref.1, s32[1,2]{1,0:T(1,128)} %val_ref.1), custom_call_target="tpu_custom_call" | custom-call | tf_op jit(solution)/shard_map/tree_attention/pallas_call | solution.py:463
  145.9 0.0 copy-start
  145.9 2.3 %copy.11 = bf16[2048,256]{1,0:T(8,128)(2,1)} copy(bf16[2048,256]{1,0:T(8,128)(2,1)} %get-tuple-element.4) | data formatting | bytes 2097152
  148.2 0.0 copy-done
  148.2 0.8 copy.12
Async XLA Ops:
  145.9 2.3 %copy-start = (bf16[2048,128]{1,0:T(8,128)(2,1)S(1)}, bf16[2048,128]{1,0:T(8,128)(2,1)}, u32[]{:S(2)}) copy-start(bf16[2048,128]{1,0:T(8,128)(2,1)} %get-tuple-element.5) | copy-start | bytes 1572868

commit v4 on v3

--- a/solution.py
+++ b/solution.py
@@ -296,6 +296,27 @@
                 wait_for(part_buf.at[slot, part(j)], yb_recv.at[slot, j])
             bown_start(u)
 
+        @when(turn & (u < n))
+        def _():
+            c = chunk_at(u)
+
+            @when(zh == 2)
+            def _():
+                right(c).wait_send()
+
+            @when(zh == 1)
+            def _():
+                left(c).wait_send()
+
+            for slot in range(2):
+                @when(y != HOME[slot])
+                def _():
+                    along_y(slot, c).wait_send()
+
+            @when(u < nhalo)
+            def _():
+                to_next(nhalo - 1 - u).wait_send()
+
         @when((t >= LANDED) & (t < n + LANDED))
         def _():
             k = t - LANDED
@@ -388,6 +409,14 @@
         @when(turn & (u >= BACK_END))
         def _():
             j = back_at(u - BACK_END)
+            for which in range(2):
+                @when(y != HOME[which])
+                def _():
+                    back_y(which, j).wait_send()
+
+            @when(u - BACK_END >= n - nhalo)
+            def _():
+                to_before(u - BACK_END - (n - nhalo)).wait_send()
 
             @when(zh <= 1)
             def _():
@@ -424,24 +453,11 @@
     def drain(k, carry):
         @when(zh == 2)
         def _():
-            right(k).wait_send()
             back_left(k).wait_send()
 
         @when(zh == 1)
         def _():
-            left(k).wait_send()
             back_right(k).wait_send()
-
-        for slot in range(2):
-            @when(y != HOME[slot])
-            def _():
-                along_y(slot, k).wait_send()
-                back_y(slot, k).wait_send()
-
-        @when(k < nhalo)
-        def _():
-            to_next(k).wait_send()
-            to_before(k).wait_send()
 
         return carry
 

time: 149 us -> 149 us (level)
  no operation moved by 1% of the time
where the time goes in v4:
time: 149 us; the launch traced here: 148 us
  Pallas kernels  145 us (97%)
  local copies, waits for them, and re-layouts  3.12 us (2%)
    pallas_call x1, Pallas kernels, on_device(): pl.pallas_call(functools.partial(kernel, ns, nh, rows), out_shape=(jax.Sh...  145 us
    unnamed x4, local copies, waits for them, and re-layouts  3.12 us

profile of v4, /device:TPU:129, one launch (start us, length us, event | category | flops | bytes accessed | tf_op | source)
XLA Modules:
  0.0 148.3 jit_solution(11338524005740481320)
XLA Ops:
  0.6 144.5 %tree_attention.1 = (bf16[2048,256]{1,0:T(8,128)(2,1)}, bf16[2048,128]{1,0:T(8,128)(2,1)}) custom-call(bf16[2048,128]{1,0:T(8,128)(2,1)} %kv_ref.1, bf16[2048,256]{1,0:T(8,128)(2,1)} %q_hbm.1, bf16[2048,256]{1,0:T(8,128)(2,1)} %up_hbm.1, s32[1,128]{1,0:T(1,128)} %bitcast.2, s32[1,128]{1,0:T(1,128)} %bitcast.3, s32[1,2]{1,0:T(1,128)} %anc_ref.1, s32[1,2]{1,0:T(1,128)} %val_ref.1), custom_call_target="tpu_custom_call" | custom-call | tf_op jit(solution)/shard_map/tree_attention/pallas_call | solution.py:479
  145.2 0.0 copy-start
  145.2 2.3 %copy.11 = bf16[2048,256]{1,0:T(8,128)(2,1)} copy(bf16[2048,256]{1,0:T(8,128)(2,1)} %get-tuple-element.4) | data formatting | bytes 2097152
  147.5 0.0 copy-done
  147.5 0.8 copy.12
Async XLA Ops:
  145.2 2.3 %copy-start = (bf16[2048,128]{1,0:T(8,128)(2,1)S(1)}, bf16[2048,128]{1,0:T(8,128)(2,1)}, u32[]{:S(2)}) copy-start(bf16[2048,128]{1,0:T(8,128)(2,1)} %get-tuple-element.5) | copy-start | bytes 1572868
